TPU v7x, 32 devices: a whole 2x2x4 slice. The times are simulated.
32 devices in a mesh: dp: 1, dap: 32 (over z, y, x, core).
Axes of the slice: x: 2, y: 2, z: 4, core: 2. Of those that a mesh axis runs over, the one named last changes fastest.
Arguments:
- alignment: bfloat16 [128, 256, 256], P(('dp', 'dap')), may hold values from -6 to 6
- pair_rep: bfloat16 [256, 256, 128], P(('dp', 'dap')), may hold values from -6 to 6
- align_mask: int32 [128, 256], P(('dp', 'dap')), may hold values 0 or 1
- residue_mask: int32 [256], P('dp'), may hold values 0 or 1
- row_gain: float32 [256], replicated, may hold values from 0.1 to 1.9
- pair_gain: float32 [128], replicated, may hold values from 0.1 to 1.9
- row_bias: bfloat16 [128, 8], replicated, may hold values from -0.5 to 0.5
- row_scoring: bfloat16 [256, 512], replicated, may hold values from -4 to 4
- row_values: bfloat16 [256, 512], replicated, may hold values from -0.375 to 0.375
- row_output: bfloat16 [256, 256], replicated, may hold values from -0.375 to 0.375
- column_gain: float32 [256], replicated, may hold values from 0.1 to 1.9
- column_scoring: bfloat16 [256, 512], replicated, may hold values from -4 to 4
- column_values: bfloat16 [256, 512], replicated, may hold values from -0.375 to 0.375
- column_output: bfloat16 [256, 256], replicated, may hold values from -0.375 to 0.375
- outer_gain: float32 [256], replicated, may hold values from 0.1 to 1.9
- outer_inputs: bfloat16 [256, 64], replicated, may hold values from -0.375 to 0.375
- outer_output: bfloat16 [1024, 128], replicated, may hold values from -1 to 1
Outputs:
- new_alignment: bfloat16 [128, 256, 256], P(('dp', 'dap'))
- new_pair: bfloat16 [256, 256, 128], P(('dp', 'dap'))
All inputs are finite; a program needn't handle non-finite values. No bound on the sum of `align_mask` on one device may be relied on, other than what follows from the above.
Results may differ from a plain program's by a relative error of at most 0.012.
The roundings to bfloat16 on the way count: a program that leaves them out, or rounds other values in their place, can miss the bound.
Values may be sent and summed in bfloat16 or wider, within the bound.
A program may use at most 64 MiB of HBM per device.

v0:
```python
import math
import jax
import jax.numpy as jnp
from jax import lax
from jax.sharding import PartitionSpec as P

HEADS = 8
HEAD = 32
C_OPM = 32


def layer_norm(values_in, gain):
    wide = values_in.astype(jnp.float32)
    average = jnp.mean(wide, axis=-1, keepdims=True)
    centred = wide - average
    spread = jnp.mean(centred * centred, axis=-1, keepdims=True)
    return (centred * lax.rsqrt(spread + 1e-05) * gain).astype(jnp.bfloat16)


def linear(inputs, weight):
    return jnp.einsum("...c,cd->...d", inputs, weight, preferred_element_type=jnp.float32)


def split_heads(tensor):
    return tensor.reshape(tensor.shape[:2] + (HEADS, HEAD))


def row_attend(queries, keys_all, values_all, gates, keep_mask, bias_term):
    scores = jnp.einsum(
        "sihd,sjhd->shij",
        split_heads(queries),
        split_heads(keys_all),
        preferred_element_type=jnp.float32,
    )
    scores = scores / math.sqrt(HEAD) + bias_term[None]
    scores = jnp.where(keep_mask[:, None, None, :] > 0, scores, -1000000000.0)
    weights = jax.nn.softmax(scores, axis=-1).astype(jnp.bfloat16)
    mixed = jnp.einsum(
        "shij,sjhd->sihd", weights, split_heads(values_all), preferred_element_type=jnp.float32
    )
    mixed = mixed.reshape(queries.shape)
    return (mixed * jax.nn.sigmoid(gates.astype(jnp.float32))).astype(jnp.bfloat16)


def column_attend(queries, keys_all, values_all, gates, keep_mask):
    scores = jnp.einsum(
        "srhd,trhd->rhst",
        split_heads(queries),
        split_heads(keys_all),
        preferred_element_type=jnp.float32,
    )
    scores = scores / math.sqrt(HEAD)
    keep_turned = jnp.swapaxes(keep_mask, 0, 1)
    scores = jnp.where(keep_turned[:, None, None, :] > 0, scores, -1000000000.0)
    weights = jax.nn.softmax(scores, axis=-1).astype(jnp.bfloat16)
    mixed = jnp.einsum(
        "rhst,trhd->srhd", weights, split_heads(values_all), preferred_element_type=jnp.float32
    )
    mixed = mixed.reshape(queries.shape)
    return (mixed * jax.nn.sigmoid(gates.astype(jnp.float32))).astype(jnp.bfloat16)


def body(
    alignment,
    pair_rep,
    align_mask,
    residue_mask,
    row_gain,
    pair_gain,
    row_bias,
    row_scoring,
    row_values,
    row_output,
    column_gain,
    column_scoring,
    column_values,
    column_output,
    outer_gain,
    outer_inputs,
    outer_output,
):
    channels = alignment.shape[2]
    rows_here = pair_rep.shape[0]
    mask_float = align_mask.astype(jnp.float32)
    mask_narrow = align_mask.astype(jnp.bfloat16)
    residue_float = residue_mask.astype(jnp.float32)
    pair_bias = jnp.einsum(
        "ijz,zh->hij", layer_norm(pair_rep, pair_gain), row_bias, preferred_element_type=jnp.float32
    ).astype(jnp.bfloat16)
    normed = layer_norm(alignment, row_gain)
    joint = linear(normed, row_scoring).astype(jnp.bfloat16)
    gated = linear(normed, row_values).astype(jnp.bfloat16)
    queries, keys_all = (joint[..., :channels], joint[..., channels:])
    values_all, gates = (gated[..., :channels], gated[..., channels:])
    keep_rows = mask_float * residue_float[None, :]
    mixed = row_attend(
        queries,
        keys_all,
        values_all,
        gates,
        keep_rows,
        lax.all_gather(pair_bias, "dap", axis=1, tiled=True).astype(jnp.float32),
    )
    row_update = linear(mixed, row_output)
    first_update = (alignment.astype(jnp.float32) + row_update).astype(jnp.bfloat16)
    columns, column_keep = (
        lax.all_to_all(first_update, "dap", split_axis=1, concat_axis=0, tiled=True),
        lax.all_to_all(mask_narrow, "dap", split_axis=1, concat_axis=0, tiled=True),
    )
    keep_columns = column_keep.astype(jnp.float32)
    column_normed = layer_norm(columns, column_gain)
    column_joint = linear(column_normed, column_scoring).astype(jnp.bfloat16)
    column_gated = linear(column_normed, column_values).astype(jnp.bfloat16)
    column_mixed = column_attend(
        column_joint[..., :channels],
        column_joint[..., channels:],
        column_gated[..., :channels],
        column_gated[..., channels:],
        keep_columns,
    )
    second_update = (columns.astype(jnp.float32) + linear(column_mixed, column_output)).astype(
        jnp.bfloat16
    )
    new_alignment = lax.all_to_all(second_update, "dap", split_axis=0, concat_axis=1, tiled=True)
    outer_normed = layer_norm(new_alignment, outer_gain)
    sides = (linear(outer_normed, outer_inputs) * mask_float[..., None]).astype(jnp.bfloat16)
    left_side = lax.all_to_all(sides[..., :C_OPM], "dap", split_axis=1, concat_axis=0, tiled=True)
    right_side, right_keep = (
        lax.all_gather(sides[..., C_OPM:], "dap", axis=0, tiled=True),
        lax.all_gather(mask_narrow, "dap", axis=0, tiled=True),
    )
    pair_count = jnp.dot(
        jnp.swapaxes(column_keep, 0, 1), right_keep, preferred_element_type=jnp.float32
    )
    total_res = right_side.shape[1]
    span = math.gcd(total_res, 128)
    block_count = total_res // span
    right_blocks = jnp.moveaxis(
        right_side.reshape(right_side.shape[0], block_count, span, C_OPM), 1, 0
    )

    def outer_block(right_piece):
        products = jnp.einsum(
            "sic,sje->ijce", left_side, right_piece, preferred_element_type=jnp.float32
        ).astype(jnp.bfloat16)
        flat = products.reshape(rows_here, span, C_OPM * C_OPM)
        return linear(flat, outer_output)

    outer_rows = lax.map(outer_block, right_blocks)
    outer_rows = jnp.moveaxis(outer_rows, 0, 1).reshape(rows_here, total_res, outer_output.shape[1])
    offset = lax.axis_index("dap") * rows_here
    row_factor = lax.dynamic_slice_in_dim(residue_float, offset, rows_here)
    scaled = (
        outer_rows
        / (0.001 + pair_count)[..., None]
        * row_factor[:, None, None]
        * residue_float[None, :, None]
    )
    new_pair = (pair_rep.astype(jnp.float32) + scaled).astype(jnp.bfloat16)
    return (new_alignment, new_pair)


def solution(mesh):
    in_specs = (
        P(("dp", "dap"), None, None),
        P(("dp", "dap"), None, None),
        P(("dp", "dap"), None),
        P("dp"),
        P(),
        P(),
        P(),
        P(),
        P(),
        P(),
        P(),
        P(),
        P(),
        P(),
        P(),
        P(),
        P(),
    )
    out_specs = (P(("dp", "dap"), None, None), P(("dp", "dap"), None, None))
    return jax.shard_map(body, mesh=mesh, in_specs=in_specs, out_specs=out_specs, check_vma=False)
```

profile of v0, /device:TPU:0, one launch (start us, length us, event | category | flops | bytes accessed | tf_op | source)
XLA Modules:
  0.0 223.3 jit_solution(6364969437507721524)
XLA Ops:
  7.2 1.3 convert_reduce_fusion
  8.5 1.7 fusion.27
  10.3 2.5 %fusion.26 = bf16[8,8,256]{2,0,1:T(8,128)(2,1)} fusion(bf16[8,256,128]{2,1,0:T(8,128)(2,1)} %param.20, f32[128]{0:T(128)} %param.24, f32[8,256]{1,0:T(8,128)S(1)} %add_rsqrt_fusion.2, f32[8,256]{1,0:T(8,128)S(1)} %broadcast_multiply_fusion.2, bf16[128,8]{0,1:T(8,128)(2,1)} %param.25), kind=kOutput, calls=%fused_computation.50 | convolution fusion | flops 5521408 | bytes 576000 | tf_op jit(solution)/shard_map/ijz,zh->hij/dot_general | solution.py:87
  14.2 7.3 %all-to-all-start.1 = ((bf16[4,32,8]{2,0,1:T(4,128)(2,1)}), bf16[4,32,8]{2,0,1:T(4,128)(2,1)S(1)}, u32[]{:S(2)}, u32[]{:S(2)}) async-start(bf16[4,32,8]{2,0,1:T(4,128)(2,1)} %copy.118), calls=%async_computation.1 | async-start | bytes 65536 | tf_op jit(solution)/shard_map/all_to_all | solution.py:108
  21.5 1.3 convert_reduce_fusion.1
  22.8 1.4 fusion.30
  24.3 1.5 convolution_convert_fusion.2
  28.8 40.5 %all-gather.4.cloned.1.call-done = bf16[8,256,256]{2,0,1:T(8,128)(2,1)} async-done(((bf16[8,8,256]{2,0,1:T(8,128)(2,1)}), bf16[8,256,256]{2,0,1:T(8,128)(2,1)}) %all-gather.4.cloned.1.call-update) | async-done | bytes 1048592 | tf_op jit(solution)/shard_map/all_gather | solution.py:102
  69.3 1.9 copy.104
  71.1 7.6 %fusion.73 = (f32[4,8,256]{2,1,0:T(8,128)S(1)}, f32[4,8,256,256]{2,3,1,0:T(8,128)}) fusion(f32[8,256,256]{1,2,0:T(8,128)S(1)} %copy.104, pred[4,256]{1,0:T(4,128)(4,1)S(1)} %multiply_compare_fusion, bf16[4,256,8,32]{1,3,2,0:T(8,128)(2,1)S(1)} %bitcast.152, bf16[4,256,8,32]{1,3,2,0:T(8,128)(2,1)} %bitcast.153), kind=kOutput, calls=%fused_computation.113 | convolution fusion | flops 144703744 | bytes 11568128 | tf_op jit(solution)/shard_map/sub | solution.py:37
  78.8 4.4 %fusion.13 = f32[4,8,32,256]{3,2,1,0:T(8,128)S(1)} fusion(bf16[4,256,8,32]{1,3,2,0:T(8,128)(2,1)} %bitcast.154, f32[4,8,256,256]{2,3,1,0:T(8,128)} %get-tuple-element.64, f32[4,8,256]{2,1,0:T(8,128)S(1)} %get-tuple-element.63), kind=kOutput, calls=%fused_computation.21 | convolution fusion | flops 138412032 | bytes 9994240 | tf_op jit(solution)/shard_map/shij,sjhd->sihd/dot_general | solution.py:38
  83.6 1.5 fusion.19
  85.0 1.2 copy.107
  86.2 3.6 %all-to-all-start = ((bf16[4,256,256]{2,0,1:T(4,128)(2,1)}), bf16[4,256,256]{2,0,1:T(4,128)(2,1)S(1)}, u32[]{:S(2)}, u32[]{:S(2)}) async-start(bf16[4,256,256]{2,0,1:T(4,128)(2,1)} %copy.107), calls=%async_computation | async-start | bytes 1048576 | tf_op jit(solution)/shard_map/all_to_all | solution.py:107
  90.1 15.2 %all-to-all-done = bf16[4,256,256]{2,0,1:T(4,128)(2,1)S(1)} async-done(((bf16[4,256,256]{2,0,1:T(4,128)(2,1)}), bf16[4,256,256]{2,0,1:T(4,128)(2,1)S(1)}, u32[]{:S(2)}, u32[]{:S(2)}) %all-to-all-start) | async-done | bytes 524320 | tf_op jit(solution)/shard_map/all_to_all | solution.py:107
  111.5 4.8 %fusion.74 = (f32[8,8,128]{2,1,0:T(8,128)S(1)}, f32[8,8,128,128]{2,3,1,0:T(8,128)}) fusion(pred[8,128]{1,0:T(8,128)(4,1)S(1)} %copy.119, bf16[128,8,8,32]{0,3,2,1:T(8,128)(2,1)S(1)} %bitcast.155, bf16[128,8,8,32]{0,3,2,1:T(8,128)(2,1)} %bitcast.156), kind=kOutput, calls=%fused_computation.114 | convolution fusion | flops 71303296 | bytes 5276672 | tf_op jit(solution)/shard_map/sub | solution.py:55
  116.3 3.0 %fusion.17 = f32[8,8,32,128]{3,2,1,0:T(8,128)S(1)} fusion(bf16[128,8,8,32]{0,3,2,1:T(8,128)(2,1)} %bitcast.157, f32[8,8,128,128]{2,3,1,0:T(8,128)} %get-tuple-element.66, f32[8,8,128]{2,1,0:T(8,128)S(1)} %get-tuple-element.65), kind=kOutput, calls=%fused_computation.26 | convolution fusion | flops 69206016 | bytes 5799936 | tf_op jit(solution)/shard_map/rhst,trhd->srhd/dot_general | solution.py:56
  119.4 1.3 copy.123
  120.7 1.7 fusion.20
  122.7 18.4 %all_to_all.64 = bf16[128,8,256]{2,1,0:T(8,128)(2,1)S(1)} all-to-all(bf16[128,8,256]{2,1,0:T(8,128)(2,1)S(1)} %copy.124), channel_id=1, replica_groups=mesh['dp'=1,'dap'=32] {'dap'}, dimensions={0} | all-to-all | bytes 1048576 | tf_op jit(solution)/shard_map/all_to_all | solution.py:124
  144.7 39.2 %all-gather = bf16[32,4,256]{2,1,0:T(4,128)(2,1)S(1)} all-gather(bf16[1,4,256]{2,1,0:T(4,128)(2,1)S(1)} %bitcast.162), channel_id=1, replica_groups=mesh['dp'=1,'dap'=32] {'dap'}, dimensions={0}, use_global_device_ids=true | all-gather | bytes 67584 | tf_op jit(solution)/shard_map/all_gather | solution.py:130
  185.0 2.8 %all-to-all-start.3 = ((bf16[32,2,512]{2,1,0:T(2,128)(2,1)}), bf16[32,2,512]{2,1,0:T(2,128)(2,1)S(1)}, u32[]{:S(2)}, u32[]{:S(2)}) async-start(bf16[32,2,512]{2,1,0:T(2,128)(2,1)} %reshape.172), calls=%async_computation.3 | async-start | bytes 131072 | tf_op jit(solution)/shard_map/all_to_all | solution.py:127
  187.9 7.5 %all-to-all-done.3 = bf16[32,2,512]{2,1,0:T(2,128)(2,1)S(1)} async-done(((bf16[32,2,512]{2,1,0:T(2,128)(2,1)}), bf16[32,2,512]{2,1,0:T(2,128)(2,1)S(1)}, u32[]{:S(2)}, u32[]{:S(2)}) %all-to-all-start.3) | async-done | bytes 65568 | tf_op jit(solution)/shard_map/all_to_all | solution.py:127
  195.9 3.8 %all-gather.6.cloned.1.call-done = bf16[128,256,32]{1,2,0:T(8,128)(2,1)} async-done(((bf16[4,256,32]{1,2,0:T(8,128)(2,1)}), bf16[128,256,32]{1,2,0:T(8,128)(2,1)}) %all-gather.6.cloned.1.call-update) | async-done | bytes 2097168 | tf_op jit(solution)/shard_map/all_gather | solution.py:129
  199.7 4.0 %reshape.154 = bf16[128,2,128,32]{2,1,3,0:T(2,128)(2,1)} reshape(bf16[128,256,32]{1,2,0:T(8,128)(2,1)} %all-gather.6.cloned.1.call-done) | data formatting | bytes 4194304 | tf_op jit(solution)/shard_map/reshape | solution.py:139
  203.7 2.9 %copy.155 = bf16[128,2,128,32]{2,0,3,1:T(8,128)(2,1)S(1)} copy(bf16[128,2,128,32]{2,1,3,0:T(2,128)(2,1)} %reshape.154) | data formatting | bytes 4194304 | tf_op jit(solution)/shard_map/reshape | solution.py:139
  206.6 7.3 %while.10 = (s32[]{:T(128)}, f32[2,8,128,128]{3,2,1,0:T(8,128)}, bf16[2,128,128,32]{2,1,3,0:T(8,128)(2,1)S(1)}, bf16[128,8,32]{0,2,1:T(8,128)(2,1)S(1)}, bf16[1024,128]{1,0:T(8,128)(2,1)S(1)}, /*index=5*/s32[]{:T(128)}) while((s32[]{:T(128)}, f32[2,8,128,128]{3,2,1,0:T(8,128)}, bf16[2,128,128,32]{2,1,3,0:T(8,128)(2,1)S(1)}, ...), condition=%wide.region_13.14_spmd, body=%wide.region_12.13_spmd.sunk | while | flops 537919488 | bytes 10289737 | solution.py:149
  207.3 1.4 copy.161
  208.7 1.6 fusion.97
  211.0 1.4 copy.161
  212.3 1.6 fusion.97
  213.9 1.3 copy.137
  (106 shorter events, 19.3 us)
Async XLA Ops:
  7.2 17.1 %copy-start = (bf16[256,512]{1,0:T(8,128)(2,1)S(1)}, bf16[256,512]{1,0:T(8,128)(2,1)}, u32[]{:S(2)}) copy-start(bf16[256,512]{1,0:T(8,128)(2,1)} %param.26) | copy-start | bytes 786436
  7.2 62.1 %all-gather.4.cloned.1.call-start = ((), (), s32[]{:S(2)}) async-start(), calls=%async_computation.4 | async-start | bytes 1081344 | tf_op jit(solution)/shard_map/all_gather | solution.py:102
  10.2 16.9 %copy-start.10 = (s32[256]{0:T(256)S(1)}, s32[256]{0:T(256)}, u32[]{:S(2)}) copy-start(s32[256]{0:T(256)} %param.22) | copy-start | bytes 3076
  10.2 16.9 %copy-start.3 = (bf16[4,256,256]{2,1,0:T(8,128)(2,1)S(1)}, bf16[4,256,256]{2,1,0:T(8,128)(2,1)}, u32[]{:S(2)}) copy-start(bf16[4,256,256]{2,1,0:T(8,128)(2,1)} %param.19) | copy-start | bytes 1572868
  10.2 16.9 %copy-start.11 = (bf16[256,512]{1,0:T(8,128)(2,1)S(1)}, bf16[256,512]{1,0:T(8,128)(2,1)}, u32[]{:S(2)}) copy-start(bf16[256,512]{1,0:T(8,128)(2,1)} %param.27) | copy-start | bytes 786436
  10.3 16.9 %copy-start.14 = (f32[256]{0:T(256)S(1)}, f32[256]{0:T(256)}, u32[]{:S(2)}) copy-start(f32[256]{0:T(256)} %param.23) | copy-start | bytes 3076
  14.2 72.0 %all-to-all-start.1 = ((bf16[4,32,8]{2,0,1:T(4,128)(2,1)}), bf16[4,32,8]{2,0,1:T(4,128)(2,1)S(1)}, u32[]{:S(2)}, u32[]{:S(2)}) async-start(bf16[4,32,8]{2,0,1:T(4,128)(2,1)} %copy.118), calls=%async_computation.1 | async-start | bytes 65536 | tf_op jit(solution)/shard_map/all_to_all | solution.py:108
  25.8 3.0 %copy-start.8 = (s32[4,256]{1,0:T(4,128)S(1)}, s32[4,256]{1,0:T(4,128)}, u32[]{:S(2)}) copy-start(s32[4,256]{1,0:T(4,128)} %param.21) | copy-start | bytes 12292
  27.6 1.2 copy-start.7
  78.8 4.8 %copy-start.12 = (bf16[256,256]{1,0:T(8,128)(2,1)S(1)}, bf16[256,256]{1,0:T(8,128)(2,1)}, u32[]{:S(2)}) copy-start(bf16[256,256]{1,0:T(8,128)(2,1)} %param.28) | copy-start | bytes 393220
  86.2 19.1 %all-to-all-start = ((bf16[4,256,256]{2,0,1:T(4,128)(2,1)}), bf16[4,256,256]{2,0,1:T(4,128)(2,1)S(1)}, u32[]{:S(2)}, u32[]{:S(2)}) async-start(bf16[4,256,256]{2,0,1:T(4,128)(2,1)} %copy.107), calls=%async_computation | async-start | bytes 1048576 | tf_op jit(solution)/shard_map/all_to_all | solution.py:107
  89.8 109.9 %all-gather.6.cloned.1.call-start = ((), (), s32[]{:S(2)}) async-start(), calls=%async_computation.5 | async-start | bytes 2162688 | tf_op jit(solution)/shard_map/all_gather | solution.py:129
  105.7 2.3 %copy-start.5 = (bf16[256,512]{1,0:T(8,128)(2,1)S(1)}, bf16[256,512]{1,0:T(8,128)(2,1)}, u32[]{:S(2)}) copy-start(bf16[256,512]{1,0:T(8,128)(2,1)} %param.30) | copy-start | bytes 786436
  105.7 2.3 %copy-start.9 = (f32[256]{0:T(256)S(1)}, f32[256]{0:T(256)}, u32[]{:S(2)}) copy-start(f32[256]{0:T(256)} %param.29) | copy-start | bytes 3076
  107.6 2.4 %copy-start.6 = (bf16[256,512]{1,0:T(8,128)(2,1)S(1)}, bf16[256,512]{1,0:T(8,128)(2,1)}, u32[]{:S(2)}) copy-start(bf16[256,512]{1,0:T(8,128)(2,1)} %param.31) | copy-start | bytes 786436
  122.3 21.1 %copy-start.13 = (bf16[256,64]{0,1:T(8,128)(2,1)S(1)}, bf16[256,64]{0,1:T(8,128)(2,1)}, u32[]{:S(2)}) copy-start(bf16[256,64]{0,1:T(8,128)(2,1)} %param.34) | copy-start | bytes 98308
  122.3 21.1 %copy-start.15 = (f32[256]{0:T(256)S(1)}, f32[256]{0:T(256)}, u32[]{:S(2)}) copy-start(f32[256]{0:T(256)} %param.33) | copy-start | bytes 3076
  143.3 52.4 %copy-start.4 = (bf16[4,32,8,256]{3,2,1,0:T(8,128)(2,1)}, bf16[4,32,8,256]{3,2,1,0:T(8,128)(2,1)S(1)}, u32[]{:S(2)}) copy-start(bf16[4,32,8,256]{3,2,1,0:T(8,128)(2,1)S(1)} %copy.157) | copy-start | bytes 1572868
  185.0 10.4 %all-to-all-start.3 = ((bf16[32,2,512]{2,1,0:T(2,128)(2,1)}), bf16[32,2,512]{2,1,0:T(2,128)(2,1)S(1)}, u32[]{:S(2)}, u32[]{:S(2)}) async-start(bf16[32,2,512]{2,1,0:T(2,128)(2,1)} %reshape.172), calls=%async_computation.3 | async-start | bytes 131072 | tf_op jit(solution)/shard_map/all_to_all | solution.py:127
  195.9 10.7 %copy-start.1 = (bf16[1024,128]{1,0:T(8,128)(2,1)S(1)}, bf16[1024,128]{1,0:T(8,128)(2,1)}, u32[]{:S(2)}) copy-start(bf16[1024,128]{1,0:T(8,128)(2,1)} %param.35) | copy-start | bytes 786436
  206.6 8.6 %copy-start.2 = (bf16[8,256,128]{2,1,0:T(8,128)(2,1)S(1)}, bf16[8,256,128]{2,1,0:T(8,128)(2,1)}, u32[]{:S(2)}) copy-start(bf16[8,256,128]{2,1,0:T(8,128)(2,1)} %param.20) | copy-start | bytes 1572868
Sparse Core Ops, SparseCore 0:
  12.9 56.3 all-gather.3
  144.7 54.9 all-gather.5
where the time goes:
time: 224 us; the launch traced here: 223 us
  waiting for transfers between devices  67 us (30%)
  blocking collectives  57.6 us (26%)
  matrix products  33.7 us (15%)
  local copies, waits for them, and re-layouts  26.9 us (12%)
  between operations  14.6 us (7%)
  starting transfers between devices  13.9 us (6%)
  other arithmetic  9.53 us (4%)
    all_gather x1, waiting for transfers between devices, body(): lax.all_gather(pair_bias, 'dap', axis=1, tiled=True).astype(jnp.float32)  40.5 us
    all_gather x1, blocking collectives, body(): lax.all_gather(mask_narrow, 'dap', axis=0, tiled=True)  39.2 us
    all_to_all x1, blocking collectives, body(): lax.all_to_all(second_update, 'dap', split_axis=0, concat_axis=1, tiled=T...  18.4 us
    all_to_all x1, waiting for transfers between devices, body(): lax.all_to_all(first_update, 'dap', split_axis=1, concat_axis=0, tiled=True)  15.2 us
    dot_general x9, matrix products, linear(): jnp.einsum('...c,cd->...d', inputs, weight, preferred_element_type=jnp.fl...  9.78 us
    sub x1, matrix products, row_attend(): weights = jax.nn.softmax(scores, axis=-1).astype(jnp.bfloat16)  7.63 us
    all_to_all x1, waiting for transfers between devices, body(): lax.all_to_all(sides[..., :C_OPM], 'dap', split_axis=1, concat_axis=0, ti...  7.48 us
    all_to_all x1, starting transfers between devices, body(): lax.all_to_all(mask_narrow, 'dap', split_axis=1, concat_axis=0, tiled=True)  7.3 us
  transfers between devices with their start and end apart: 5, of which 4 were waited for; matrix products, arithmetic and copies ran while one was open for 12% of the time, Pallas kernels for 0%

commit v1 on v0

--- a/solution.py
+++ b/solution.py
@@ -124,7 +124,15 @@
     new_alignment = lax.all_to_all(second_update, "dap", split_axis=0, concat_axis=1, tiled=True)
     outer_normed = layer_norm(new_alignment, outer_gain)
     sides = (linear(outer_normed, outer_inputs) * mask_float[..., None]).astype(jnp.bfloat16)
-    left_side = lax.all_to_all(sides[..., :C_OPM], "dap", split_axis=1, concat_axis=0, tiled=True)
+    left_side = jnp.concatenate(
+        jax.lax.all_to_all(
+            jnp.stack(jnp.split(sides[..., :C_OPM], jax.lax.axis_size("dap"), axis=1), axis=0),
+            axis_name="dap",
+            split_axis=0,
+            concat_axis=0,
+        ),
+        axis=0,
+    )
     right_side, right_keep = (
         lax.all_gather(sides[..., C_OPM:], "dap", axis=0, tiled=True),
         lax.all_gather(mask_narrow, "dap", axis=0, tiled=True),

time: 224 us -> 253 us (1.13)
  waiting for transfers between devices: 67 us -> 102 us
  blocking collectives: 57.6 us -> 43.8 us
  local copies, waits for them, and re-layouts: 26.9 us -> 30.8 us
  starting transfers between devices: 13.9 us -> 17 us
    all_gather x1, waiting for transfers between devices: 3.78 us -> 39.3 us  [body(): lax.all_gather(sides[..., C_OPM:], 'dap', axis=0, tiled=True)]
    all_to_all x1 -> x0, blocking collectives: 18.4 us -> none  [body(): lax.all_to_all(second_update, 'dap', split_axis=0, concat_axis=1, tiled=T...]
    all_gather x1, blocking collectives: 39.2 us -> 43.8 us  [body(): lax.all_gather(mask_narrow, 'dap', axis=0, tiled=True)]
    another operation x0 -> x35, local copies, waits for them, and re-layouts: none -> 3.13 us  [body(): jnp.stack(jnp.split(sides[..., :C_OPM], jax.lax.axis_size('dap'), axis=1)...]
    all_to_all x1 -> x2, starting transfers between devices: 2.79 us -> 5.86 us  [the longest x1 3.08 us: body(): lax.all_to_all(second_update, 'dap', split_axis=0, concat_axis=1, tiled=T...]
    all_to_all x1 -> x2, waiting for transfers between devices: 7.48 us -> 7.06 us  [the longest x1 7.06 us: body(): jax.lax.all_to_all(jnp.stack(jnp.split(sides[..., :C_OPM], jax.lax.axis_s...]
  transfers between devices with their start and end apart: 5 -> 6, of which waited for: 4 -> 4; matrix products, arithmetic and copies ran while one was open for 12% -> 12% of each run, Pallas kernels for 0% -> 0%
where the time goes in v1:
time: 253 us; the launch traced here: 252 us
  waiting for transfers between devices  102 us (40%)
  blocking collectives  43.8 us (17%)
  matrix products  33.7 us (13%)
  local copies, waits for them, and re-layouts  30.8 us (12%)
  starting transfers between devices  17 us (7%)
  between operations  14.7 us (6%)
  other arithmetic  9.53 us (4%)
    all_gather x1, blocking collectives, body(): lax.all_gather(mask_narrow, 'dap', axis=0, tiled=True)  43.8 us
    all_gather x1, waiting for transfers between devices, body(): lax.all_gather(pair_bias, 'dap', axis=1, tiled=True).astype(jnp.float32)  40.5 us
    all_gather x1, waiting for transfers between devices, body(): lax.all_gather(sides[..., C_OPM:], 'dap', axis=0, tiled=True)  39.3 us
    all_to_all x1, waiting for transfers between devices, body(): lax.all_to_all(first_update, 'dap', split_axis=1, concat_axis=0, tiled=True)  15.3 us
    dot_general x9, matrix products, linear(): jnp.einsum('...c,cd->...d', inputs, weight, preferred_element_type=jnp.fl...  9.77 us
    sub x1, matrix products, row_attend(): weights = jax.nn.softmax(scores, axis=-1).astype(jnp.bfloat16)  7.63 us
    all_to_all x1, starting transfers between devices, body(): lax.all_to_all(mask_narrow, 'dap', split_axis=1, concat_axis=0, tiled=True)  7.3 us
    all_to_all x1, waiting for transfers between devices, body(): jax.lax.all_to_all(jnp.stack(jnp.split(sides[..., :C_OPM], jax.lax.axis_s...  7.06 us
  transfers between devices with their start and end apart: 6, of which 4 were waited for; matrix products, arithmetic and copies ran while one was open for 12% of the time, Pallas kernels for 0%

profile of v1, /device:TPU:0, one launch (start us, length us, event | category | flops | bytes accessed | tf_op | source)
XLA Modules:
  0.0 251.7 jit_solution(14338894560495986353)
XLA Ops:
  7.2 1.3 convert_reduce_fusion
  8.5 1.7 fusion.27
  10.3 2.5 fusion.26
  14.3 7.3 %all-to-all-start.1 = ((bf16[4,32,8]{2,0,1:T(4,128)(2,1)}), bf16[4,32,8]{2,0,1:T(4,128)(2,1)S(1)}, u32[]{:S(2)}, u32[]{:S(2)}) async-start(bf16[4,32,8]{2,0,1:T(4,128)(2,1)} %copy.145), calls=%async_computation.1 | async-start | bytes 65536 | tf_op jit(solution)/shard_map/all_to_all | solution.py:108
  21.6 1.3 convert_reduce_fusion.1
  22.9 1.4 fusion.30
  24.3 1.5 convolution_convert_fusion.2
  28.8 40.5 %all-gather.4.cloned.1.call-done = bf16[8,256,256]{2,0,1:T(8,128)(2,1)} async-done(((bf16[8,8,256]{2,0,1:T(8,128)(2,1)}), bf16[8,256,256]{2,0,1:T(8,128)(2,1)}) %all-gather.4.cloned.1.call-update) | async-done | bytes 1048592 | tf_op jit(solution)/shard_map/all_gather | solution.py:102
  69.3 1.9 copy.131
  71.2 7.6 %fusion.72 = (f32[4,8,256]{2,1,0:T(8,128)S(1)}, f32[4,8,256,256]{2,3,1,0:T(8,128)}) fusion(f32[8,256,256]{1,2,0:T(8,128)S(1)} %copy.131, pred[4,256]{1,0:T(4,128)(4,1)S(1)} %multiply_compare_fusion, bf16[4,256,8,32]{1,3,2,0:T(8,128)(2,1)S(1)} %bitcast.206, bf16[4,256,8,32]{1,3,2,0:T(8,128)(2,1)} %bitcast.207), kind=kOutput, calls=%fused_computation.175 | convolution fusion | flops 144703744 | bytes 11568128 | tf_op jit(solution)/shard_map/sub | solution.py:37
  78.8 4.4 %fusion.13 = f32[4,8,32,256]{3,2,1,0:T(8,128)S(1)} fusion(bf16[4,256,8,32]{1,3,2,0:T(8,128)(2,1)} %bitcast.208, f32[4,8,256,256]{2,3,1,0:T(8,128)} %get-tuple-element.99, f32[4,8,256]{2,1,0:T(8,128)S(1)} %get-tuple-element.98), kind=kOutput, calls=%fused_computation.21 | convolution fusion | flops 138412032 | bytes 9994240 | tf_op jit(solution)/shard_map/shij,sjhd->sihd/dot_general | solution.py:38
  83.6 1.5 fusion.19
  85.1 1.2 copy.134
  86.3 3.7 %all-to-all-start = ((bf16[4,256,256]{2,0,1:T(4,128)(2,1)}), bf16[4,256,256]{2,0,1:T(4,128)(2,1)S(1)}, u32[]{:S(2)}, u32[]{:S(2)}) async-start(bf16[4,256,256]{2,0,1:T(4,128)(2,1)} %copy.134), calls=%async_computation | async-start | bytes 1048576 | tf_op jit(solution)/shard_map/all_to_all | solution.py:107
  90.1 15.3 %all-to-all-done = bf16[4,256,256]{2,0,1:T(4,128)(2,1)S(1)} async-done(((bf16[4,256,256]{2,0,1:T(4,128)(2,1)}), bf16[4,256,256]{2,0,1:T(4,128)(2,1)S(1)}, u32[]{:S(2)}, u32[]{:S(2)}) %all-to-all-start) | async-done | bytes 524320 | tf_op jit(solution)/shard_map/all_to_all | solution.py:107
  111.5 4.8 %fusion.73 = (f32[8,8,128]{2,1,0:T(8,128)S(1)}, f32[8,8,128,128]{2,3,1,0:T(8,128)}) fusion(pred[8,128]{1,0:T(8,128)(4,1)S(1)} %copy.146, bf16[128,8,8,32]{0,3,2,1:T(8,128)(2,1)S(1)} %bitcast.209, bf16[128,8,8,32]{0,3,2,1:T(8,128)(2,1)} %bitcast.210), kind=kOutput, calls=%fused_computation.176 | convolution fusion | flops 71303296 | bytes 5276672 | tf_op jit(solution)/shard_map/sub | solution.py:55
  116.3 3.0 %fusion.17 = f32[8,8,32,128]{3,2,1,0:T(8,128)S(1)} fusion(bf16[128,8,8,32]{0,3,2,1:T(8,128)(2,1)} %bitcast.211, f32[8,8,128,128]{2,3,1,0:T(8,128)} %get-tuple-element.101, f32[8,8,128]{2,1,0:T(8,128)S(1)} %get-tuple-element.100), kind=kOutput, calls=%fused_computation.26 | convolution fusion | flops 69206016 | bytes 5799936 | tf_op jit(solution)/shard_map/rhst,trhd->srhd/dot_general | solution.py:56
  119.4 1.3 copy.150
  120.7 1.7 fusion.20
  123.5 3.1 %all-to-all-start.2 = ((bf16[128,8,256]{2,1,0:T(8,128)(2,1)}), bf16[128,8,256]{2,1,0:T(8,128)(2,1)S(1)}, u32[]{:S(2)}, u32[]{:S(2)}) async-start(bf16[128,8,256]{2,1,0:T(8,128)(2,1)} %copy.151), calls=%async_computation.2 | async-start | bytes 1048576 | tf_op jit(solution)/shard_map/all_to_all | solution.py:124
  126.7 43.8 %all-gather = bf16[32,4,256]{2,1,0:T(4,128)(2,1)S(1)} all-gather(bf16[1,4,256]{2,1,0:T(4,128)(2,1)S(1)} %bitcast.216), channel_id=1, replica_groups=mesh['dp'=1,'dap'=32] {'dap'}, dimensions={0}, use_global_device_ids=true | all-gather | bytes 67584 | tf_op jit(solution)/shard_map/all_gather | solution.py:138
  178.4 2.8 %all-to-all-start.3 = ((bf16[32,2,512]{2,1,0:T(2,128)(2,1)}), bf16[32,2,512]{2,1,0:T(2,128)(2,1)S(1)}, u32[]{:S(2)}, u32[]{:S(2)}) async-start(bf16[32,2,512]{2,1,0:T(2,128)(2,1)} %reshape.176), calls=%async_computation.3 | async-start | bytes 131072 | tf_op jit(solution)/shard_map/all_to_all | solution.py:128
  181.4 7.1 %all-to-all-done.3 = bf16[32,2,512]{2,1,0:T(2,128)(2,1)S(1)} async-done(((bf16[32,2,512]{2,1,0:T(2,128)(2,1)}), bf16[32,2,512]{2,1,0:T(2,128)(2,1)S(1)}, u32[]{:S(2)}, u32[]{:S(2)}) %all-to-all-start.3) | async-done | bytes 65568 | tf_op jit(solution)/shard_map/all_to_all | solution.py:128
  188.8 39.3 %all-gather.6.cloned.1.call-done = bf16[128,256,32]{1,2,0:T(8,128)(2,1)} async-done(((bf16[4,256,32]{1,2,0:T(8,128)(2,1)}), bf16[128,256,32]{1,2,0:T(8,128)(2,1)}) %all-gather.6.cloned.1.call-update) | async-done | bytes 2097168 | tf_op jit(solution)/shard_map/all_gather | solution.py:137
  228.2 4.0 %reshape.157 = bf16[128,2,128,32]{2,1,3,0:T(2,128)(2,1)} reshape(bf16[128,256,32]{1,2,0:T(8,128)(2,1)} %all-gather.6.cloned.1.call-done) | data formatting | bytes 4194304 | tf_op jit(solution)/shard_map/reshape | solution.py:147
  232.1 2.9 %copy.210 = bf16[128,2,128,32]{2,0,3,1:T(8,128)(2,1)S(1)} copy(bf16[128,2,128,32]{2,1,3,0:T(2,128)(2,1)} %reshape.157) | data formatting | bytes 4194304 | tf_op jit(solution)/shard_map/reshape | solution.py:147
  235.1 7.3 %while.10 = (s32[]{:T(128)}, f32[2,8,128,128]{3,2,1,0:T(8,128)}, bf16[2,128,128,32]{2,1,3,0:T(8,128)(2,1)S(1)}, bf16[128,8,32]{0,2,1:T(8,128)(2,1)S(1)}, bf16[1024,128]{1,0:T(8,128)(2,1)S(1)}, /*index=5*/s32[]{:T(128)}) while((s32[]{:T(128)}, f32[2,8,128,128]{3,2,1,0:T(8,128)}, bf16[2,128,128,32]{2,1,3,0:T(8,128)(2,1)S(1)}, ...), condition=%wide.region_13.14_spmd, body=%wide.region_12.13_spmd.sunk | while | flops 537919488 | bytes 10289737 | solution.py:157
  235.8 1.4 copy.215
  237.1 1.6 fusion.96
  239.4 1.4 copy.215
  240.8 1.6 fusion.96
  242.3 1.3 copy.193
  (170 shorter events, 23.0 us)
Async XLA Ops:
  7.2 17.1 %copy-start = (bf16[256,512]{1,0:T(8,128)(2,1)S(1)}, bf16[256,512]{1,0:T(8,128)(2,1)}, u32[]{:S(2)}) copy-start(bf16[256,512]{1,0:T(8,128)(2,1)} %param.26) | copy-start | bytes 786436
  7.2 62.1 %all-gather.4.cloned.1.call-start = ((), (), s32[]{:S(2)}) async-start(), calls=%async_computation.4 | async-start | bytes 1081344 | tf_op jit(solution)/shard_map/all_gather | solution.py:102
  10.2 16.9 %copy-start.10 = (s32[256]{0:T(256)S(1)}, s32[256]{0:T(256)}, u32[]{:S(2)}) copy-start(s32[256]{0:T(256)} %param.22) | copy-start | bytes 3076
  10.2 16.9 %copy-start.3 = (bf16[4,256,256]{2,1,0:T(8,128)(2,1)S(1)}, bf16[4,256,256]{2,1,0:T(8,128)(2,1)}, u32[]{:S(2)}) copy-start(bf16[4,256,256]{2,1,0:T(8,128)(2,1)} %param.19) | copy-start | bytes 1572868
  10.2 16.9 %copy-start.11 = (bf16[256,512]{1,0:T(8,128)(2,1)S(1)}, bf16[256,512]{1,0:T(8,128)(2,1)}, u32[]{:S(2)}) copy-start(bf16[256,512]{1,0:T(8,128)(2,1)} %param.27) | copy-start | bytes 786436
  10.3 16.9 %copy-start.14 = (f32[256]{0:T(256)S(1)}, f32[256]{0:T(256)}, u32[]{:S(2)}) copy-start(f32[256]{0:T(256)} %param.23) | copy-start | bytes 3076
  14.3 72.0 %all-to-all-start.1 = ((bf16[4,32,8]{2,0,1:T(4,128)(2,1)}), bf16[4,32,8]{2,0,1:T(4,128)(2,1)S(1)}, u32[]{:S(2)}, u32[]{:S(2)}) async-start(bf16[4,32,8]{2,0,1:T(4,128)(2,1)} %copy.145), calls=%async_computation.1 | async-start | bytes 65536 | tf_op jit(solution)/shard_map/all_to_all | solution.py:108
  25.8 3.0 %copy-start.8 = (s32[4,256]{1,0:T(4,128)S(1)}, s32[4,256]{1,0:T(4,128)}, u32[]{:S(2)}) copy-start(s32[4,256]{1,0:T(4,128)} %param.21) | copy-start | bytes 12292
  27.7 1.2 copy-start.7
  78.8 4.8 %copy-start.12 = (bf16[256,256]{1,0:T(8,128)(2,1)S(1)}, bf16[256,256]{1,0:T(8,128)(2,1)}, u32[]{:S(2)}) copy-start(bf16[256,256]{1,0:T(8,128)(2,1)} %param.28) | copy-start | bytes 393220
  86.3 19.1 %all-to-all-start = ((bf16[4,256,256]{2,0,1:T(4,128)(2,1)}), bf16[4,256,256]{2,0,1:T(4,128)(2,1)S(1)}, u32[]{:S(2)}, u32[]{:S(2)}) async-start(bf16[4,256,256]{2,0,1:T(4,128)(2,1)} %copy.134), calls=%async_computation | async-start | bytes 1048576 | tf_op jit(solution)/shard_map/all_to_all | solution.py:107
  105.8 2.3 copy-start.5
  105.8 2.3 copy-start.9
  107.6 2.4 copy-start.6
  122.3 50.5 %copy-start.13 = (bf16[256,64]{0,1:T(8,128)(2,1)S(1)}, bf16[256,64]{0,1:T(8,128)(2,1)}, u32[]{:S(2)}) copy-start(bf16[256,64]{0,1:T(8,128)(2,1)} %param.34) | copy-start | bytes 98308
  122.4 50.5 %copy-start.15 = (f32[256]{0:T(256)S(1)}, f32[256]{0:T(256)}, u32[]{:S(2)}) copy-start(f32[256]{0:T(256)} %param.33) | copy-start | bytes 3076
  123.5 47.1 %all-to-all-start.2 = ((bf16[128,8,256]{2,1,0:T(8,128)(2,1)}), bf16[128,8,256]{2,1,0:T(8,128)(2,1)S(1)}, u32[]{:S(2)}, u32[]{:S(2)}) async-start(bf16[128,8,256]{2,1,0:T(8,128)(2,1)} %copy.151), calls=%async_computation.2 | async-start | bytes 1048576 | tf_op jit(solution)/shard_map/all_to_all | solution.py:124
  126.5 101.6 %all-gather.6.cloned.1.call-start = ((), (), s32[]{:S(2)}) async-start(), calls=%async_computation.5 | async-start | bytes 2162688 | tf_op jit(solution)/shard_map/all_gather | solution.py:137
  172.8 55.4 %copy-start.4 = (bf16[4,32,8,256]{3,2,1,0:T(8,128)(2,1)}, bf16[4,32,8,256]{3,2,1,0:T(8,128)(2,1)S(1)}, u32[]{:S(2)}) copy-start(bf16[4,32,8,256]{3,2,1,0:T(8,128)(2,1)S(1)} %copy.212) | copy-start | bytes 1572868
  178.4 10.0 %all-to-all-start.3 = ((bf16[32,2,512]{2,1,0:T(2,128)(2,1)}), bf16[32,2,512]{2,1,0:T(2,128)(2,1)S(1)}, u32[]{:S(2)}, u32[]{:S(2)}) async-start(bf16[32,2,512]{2,1,0:T(2,128)(2,1)} %reshape.176), calls=%async_computation.3 | async-start | bytes 131072 | tf_op jit(solution)/shard_map/all_to_all | solution.py:128
  188.8 46.2 %copy-start.1 = (bf16[1024,128]{1,0:T(8,128)(2,1)S(1)}, bf16[1024,128]{1,0:T(8,128)(2,1)}, u32[]{:S(2)}) copy-start(bf16[1024,128]{1,0:T(8,128)(2,1)} %param.35) | copy-start | bytes 786436
  235.1 8.6 %copy-start.2 = (bf16[8,256,128]{2,1,0:T(8,128)(2,1)S(1)}, bf16[8,256,128]{2,1,0:T(8,128)(2,1)}, u32[]{:S(2)}) copy-start(bf16[8,256,128]{2,1,0:T(8,128)(2,1)} %param.20) | copy-start | bytes 1572868
Sparse Core Ops, SparseCore 0:
  12.9 56.3 all-gather.3
  174.2 53.9 all-gather.5
